TPU v7x, 32 devices: a whole 2x2x4 slice. The times are simulated.
32 devices in a mesh: expert: 4 (over z), tensor: 8 (over y, x, core).
Axes of the slice: x: 2, y: 2, z: 4, core: 2. Of those that a mesh axis runs over, the one named last changes fastest.
Arguments:
- activations: bfloat16 [3072, 512], P('tensor', 'expert'), may hold values from -6 to 6
- cotangent: bfloat16 [3072, 512], P('tensor', 'expert'), may hold values from -4 to 4
- route_ids: int32 [512, 2], P('expert'), may hold values from 0 to 3, all different within a row; in each aligned block of 128 rows (0 to 127, 128 to 255, ...) at most 80 rows name the same one
- gate_probs: float32 [512, 2], P('expert'), may hold values from 0.2 to 0.8
- gate_weight: bfloat16 [4, 3072, 16384], P('expert', None, 'tensor'), may hold values from -0.15625 to 0.15625
- up_weight: bfloat16 [4, 3072, 16384], P('expert', None, 'tensor'), may hold values from -0.15625 to 0.15625
- down_weight: bfloat16 [4, 16384, 3072], P('expert', 'tensor'), may hold values from -0.046875 to 0.046875
Outputs:
- grad_input: bfloat16 [3072, 512], P('tensor', 'expert')
- score_grad: float32 [512, 2], P('expert')
Inputs may be any that keep to these rules, and one draw needn't show every extreme that they name: `route_ids`: each token names 2 different experts. Among the 128 tokens of one index of the expert axis no expert is named more than 80 times, and in every draw some such block names one expert exactly 80 times.
All inputs are finite; a program needn't handle non-finite values.
Results may differ from a plain program's by a relative error of at most 0.008.
Values may be sent and summed in bfloat16 or wider, within the bound.
A program may use at most 128 MiB of HBM per device.

v0:
```python
import jax
import jax.numpy as jnp
from jax import lax
from jax.sharding import PartitionSpec as P

EXTRA_ROWS = 16


def slot_numbers(route_ids, expert_count, capacity):
    token_count = route_ids.shape[0]
    onehot = route_ids[:, :, None] == jnp.arange(expert_count, dtype=jnp.int32)[None, None, :]
    named = jnp.sum(onehot.astype(jnp.float32), axis=1).astype(jnp.bfloat16)
    order = jnp.arange(token_count, dtype=jnp.int32)
    before = (order[None, :] < order[:, None]).astype(jnp.bfloat16)
    earlier = jnp.dot(before, named, preferred_element_type=jnp.float32)
    position = jnp.sum(jnp.where(onehot, earlier[:, None, :], 0.0), axis=2).astype(jnp.int32)
    return route_ids * capacity + position


def swiglu_backward(gate_sum, up_sum, hidden_grad):
    sigma = jax.nn.sigmoid(gate_sum)
    silu_value = gate_sum * sigma
    grad_up = (hidden_grad * silu_value).astype(jnp.bfloat16)
    grad_gate = (hidden_grad * up_sum * sigma * (1.0 + gate_sum * (1.0 - sigma))).astype(
        jnp.bfloat16
    )
    score_rows = jnp.sum(silu_value * up_sum * hidden_grad, axis=1)
    return (grad_gate, grad_up, score_rows)


def body(activations, cotangent, route_ids, gate_probs, gate_weight, up_weight, down_weight):
    expert_count = lax.axis_size("expert")
    tokens_here = route_ids.shape[0]
    capacity = min(tokens_here, 5 * tokens_here // (2 * expert_count))
    slot_total = expert_count * capacity
    destination = slot_numbers(route_ids, expert_count, capacity)
    slot_range = jnp.arange(slot_total, dtype=jnp.int32)
    matches = destination[:, :, None] == slot_range[None, None, :]
    placing = jnp.sum(matches.astype(jnp.float32), axis=1).astype(jnp.bfloat16)
    weighting = jnp.sum(jnp.where(matches, gate_probs[:, :, None], jnp.float32(0.0)), axis=1)
    gate_local = gate_weight[0]
    up_local = up_weight[0]
    down_local = down_weight[0]
    first_dims = (((0,), (0,)), ((), ()))
    down_dims = (((0,), (1,)), ((), ()))
    hidden_dims = (((1,), (1,)), ((), ()))
    features_here = activations.shape[0]
    send_in = jnp.dot(activations, placing, preferred_element_type=jnp.float32).astype(jnp.bfloat16)
    send_grad = jnp.dot(cotangent, placing, preferred_element_type=jnp.float32).astype(jnp.bfloat16)
    recv_in, recv_grad = (
        lax.all_to_all(send_in, "expert", split_axis=1, concat_axis=1, tiled=True),
        lax.all_to_all(send_grad, "expert", split_axis=1, concat_axis=1, tiled=True),
    )
    feature_piece = lax.all_gather(recv_in, "tensor", axis=0, tiled=True)
    grad_piece = lax.all_gather(recv_grad, "tensor", axis=0, tiled=True)
    gate_rows = gate_local
    up_rows = up_local
    gate_sum = lax.dot_general(
        feature_piece, gate_rows, first_dims, preferred_element_type=jnp.float32
    )
    up_sum = lax.dot_general(feature_piece, up_rows, first_dims, preferred_element_type=jnp.float32)
    hidden_grad = lax.dot_general(
        grad_piece, down_local, down_dims, preferred_element_type=jnp.float32
    )
    gate_sum, up_sum, hidden_grad = (gate_sum, up_sum, hidden_grad)
    grad_gate, grad_up, score_rows = swiglu_backward(gate_sum, up_sum, hidden_grad)
    gate_rows = gate_local
    up_rows = up_local
    term = lax.dot_general(gate_rows, grad_gate, hidden_dims, preferred_element_type=jnp.float32)
    term = term + lax.dot_general(up_rows, grad_up, hidden_dims, preferred_element_type=jnp.float32)
    tensor_count = lax.axis_size("tensor")
    score_high = score_rows.astype(jnp.bfloat16)
    score_low = (score_rows - score_high.astype(jnp.float32)).astype(jnp.bfloat16)
    extra = jnp.concatenate(
        [
            score_high[None, :],
            score_low[None, :],
            jnp.zeros((EXTRA_ROWS - 2, slot_total), jnp.bfloat16),
        ],
        axis=0,
    )
    blocks = term.astype(jnp.bfloat16).reshape(tensor_count, features_here, slot_total)
    extra = jnp.broadcast_to(extra[None], (tensor_count, EXTRA_ROWS, slot_total))
    parts = lax.all_to_all(
        jnp.concatenate([blocks, extra], axis=1), "tensor", split_axis=0, concat_axis=0, tiled=True
    ).astype(jnp.float32)
    totals = jnp.sum(parts, axis=0)
    score = (
        totals[features_here : features_here + 1] + totals[features_here + 1 : features_here + 2]
    )
    score_high = score.astype(jnp.bfloat16)
    score_low = (score - score_high.astype(jnp.float32)).astype(jnp.bfloat16)
    summed = jnp.concatenate(
        [
            totals[:features_here].astype(jnp.bfloat16),
            score_high,
            score_low,
            jnp.zeros((EXTRA_ROWS - 2, slot_total), jnp.bfloat16),
        ],
        axis=0,
    )
    back = lax.all_to_all(summed, "expert", split_axis=1, concat_axis=1, tiled=True)
    back = back.astype(jnp.float32)
    back_terms = back[:features_here]
    back_scores = (
        back[features_here : features_here + 1] + back[features_here + 1 : features_here + 2]
    )
    grad_local = jnp.dot(
        back_terms, weighting.T, precision=lax.Precision.HIGHEST, preferred_element_type=jnp.float32
    )
    score_grad = jnp.sum(
        jnp.where(matches, back_scores[0][None, None, :], jnp.float32(0.0)), axis=2
    )
    grad_input = grad_local.astype(jnp.bfloat16)
    return (grad_input, score_grad)


def solution(mesh):
    in_specs = (
        P("tensor", "expert"),
        P("tensor", "expert"),
        P("expert", None),
        P("expert", None),
        P("expert", None, "tensor"),
        P("expert", None, "tensor"),
        P("expert", "tensor", None),
    )
    out_specs = (P("tensor", "expert"), P("expert", None))
    return jax.shard_map(body, mesh=mesh, in_specs=in_specs, out_specs=out_specs, check_vma=False)
```

profile of v0, /device:TPU:0, one launch (start us, length us, event | category | flops | bytes accessed | tf_op | source)
XLA Modules:
  0.0 178.5 jit_solution(15263084820237573660)
XLA Ops:
  7.2 0.0 copy-start
  7.2 0.0 all-gather.5.cloned.1.call-start
  7.2 0.7 convert_reduce_fusion.2
  7.9 0.1 fusion.23
  8.1 0.7 select_reduce_fusion.2
  8.8 0.7 convert_add_fusion
  9.5 0.0 copy-done
  9.5 0.2 convolution_convert_fusion
  9.8 14.7 %all_to_all.38 = bf16[384,4,80]{0,2,1:T(8,128)(2,1)} all-to-all(bf16[384,4,80]{0,2,1:T(8,128)(2,1)S(1)} %bitcast.50), channel_id=1, replica_groups=mesh['expert'=4,'tensor'=8] {'expert'}, dimensions={1} | all-to-all | bytes 491520 | tf_op jit(solution)/shard_map/all_to_all | solution.py:51
  24.5 0.0 all-gather.5.cloned.1.call-update
  24.5 0.0 all-gather.3.cloned.1.call-start
  24.6 1.1 convolution_convert_fusion.1
  25.7 10.7 %all_to_all.39 = bf16[384,4,80]{0,2,1:T(8,128)(2,1)} all-to-all(bf16[384,4,80]{0,2,1:T(8,128)(2,1)S(1)} %bitcast.49), channel_id=1, replica_groups=mesh['expert'=4,'tensor'=8] {'expert'}, dimensions={1} | all-to-all | bytes 491520 | tf_op jit(solution)/shard_map/all_to_all | solution.py:52
  36.5 0.0 all-gather.3.cloned.1.call-update
  36.5 14.9 %all-gather.5.cloned.1.call-done = bf16[3072,320]{0,1:T(8,128)(2,1)} async-done(((bf16[384,320]{0,1:T(8,128)(2,1)}), bf16[3072,320]{0,1:T(8,128)(2,1)}) %all-gather.5.cloned.1.call-update) | async-done | bytes 1966096 | tf_op jit(solution)/shard_map/all_gather | solution.py:54
  51.4 0.0 copy-start.3
  51.4 9.4 %fusion.2 = f32[320,2048]{1,0:T(8,128)S(1)} fusion(bf16[3072,320]{0,1:T(8,128)(2,1)} %all-gather.5.cloned.1.call-done, bf16[1,3072,2048]{2,1,0:T(8,128)(2,1)} %param.11), kind=kOutput, calls=%fused_computation.2 | convolution fusion | flops 4026531840 | bytes 17170432 | tf_op jit(solution)/shard_map/dot_general | solution.py:58
  60.8 0.0 copy-done.3
  60.8 8.8 %fusion.6 = f32[320,2048]{1,0:T(8,128)} fusion(bf16[3072,320]{0,1:T(8,128)(2,1)S(1)} %copy-done.3, bf16[1,3072,2048]{2,1,0:T(8,128)(2,1)} %param.12), kind=kOutput, calls=%fused_computation.6 | convolution fusion | flops 4026531840 | bytes 17170432 | tf_op jit(solution)/shard_map/dot_general | solution.py:61
  69.6 11.3 %all-gather.3.cloned.1.call-done = bf16[3072,320]{0,1:T(8,128)(2,1)} async-done(((bf16[384,320]{0,1:T(8,128)(2,1)}), bf16[3072,320]{0,1:T(8,128)(2,1)}) %all-gather.3.cloned.1.call-update) | async-done | bytes 1966096 | tf_op jit(solution)/shard_map/all_gather | solution.py:55
  80.9 12.0 %multiply_reduce_fusion = (f32[320]{0:T(512)S(1)}, f32[320,2048]{1,0:T(8,128)}) fusion(f32[320,2048]{1,0:T(8,128)} %fusion.6, f32[320,2048]{1,0:T(8,128)S(1)} %fusion.2, bf16[3072,320]{0,1:T(8,128)(2,1)} %all-gather.3.cloned.1.call-done, bf16[1,2048,3072]{2,1,0:T(8,128)(2,1)} %param.13), kind=kOutput, calls=%fused_computation.14 | convolution fusion | flops 4031119104 | bytes 22414592 | tf_op jit(solution)/shard_map/dot_general | solution.py:62
  93.0 12.8 %fusion = f32[320,3072]{1,0:T(8,128)} fusion(bf16[1,3072,2048]{2,1,0:T(8,128)(2,1)} %param.11, f32[320,2048]{1,0:T(8,128)S(1)} %fusion.2, f32[320,2048]{1,0:T(8,128)} %get-tuple-element.7, f32[320,2048]{1,0:T(8,128)} %fusion.6), kind=kOutput, calls=%fused_computation | convolution fusion | flops 4033085440 | bytes 24379392 | tf_op jit(solution)/shard_map/dot_general | solution.py:69
  105.8 12.1 %fusion.16 = bf16[3072,320]{0,1:T(8,128)(2,1)} fusion(f32[320,3072]{1,0:T(8,128)} %fusion, bf16[1,3072,2048]{2,1,0:T(8,128)(2,1)} %param.12, f32[320,2048]{1,0:T(8,128)} %get-tuple-element.7, f32[320,2048]{1,0:T(8,128)S(1)} %fusion.2), kind=kOutput, calls=%fused_computation.13 | convolution fusion | flops 4032430080 | bytes 23724032 | tf_op jit(solution)/shard_map/dot_general | solution.py:70
  117.9 2.9 %copy.40 = bf16[3072,320]{1,0:T(8,128)(2,1)S(1)} copy(bf16[3072,320]{0,1:T(8,128)(2,1)} %fusion.16) | data formatting | bytes 3932160 | tf_op jit(solution)/shard_map/reshape | solution.py:82
  120.9 0.3 pad_maximum_fusion
  121.1 33.0 %all_to_all.40 = bf16[8,400,320]{2,1,0:T(8,128)(2,1)S(1)} all-to-all(bf16[8,400,320]{2,1,0:T(8,128)(2,1)S(1)} %pad_maximum_fusion), channel_id=1, replica_groups=mesh['expert'=4,'tensor'=8] {'tensor'}, dimensions={0} | all-to-all | bytes 4096000 | tf_op jit(solution)/shard_map/all_to_all | solution.py:84
  154.1 0.0 copy-start.1
  154.1 0.4 convert_reduce_fusion
  154.5 0.0 copy-start.2
  154.7 0.2 copy.39
  154.8 14.5 %all_to_all.41 = bf16[400,4,80]{0,2,1:T(8,128)(2,1)S(1)} all-to-all(bf16[400,4,80]{0,2,1:T(8,128)(2,1)S(1)} %bitcast.45), channel_id=1, replica_groups=mesh['expert'=4,'tensor'=8] {'expert'}, dimensions={1} | all-to-all | bytes 512000 | tf_op jit(solution)/shard_map/all_to_all | solution.py:102
  169.3 0.1 convert_element_type.115
  169.4 0.2 fusion.22
  169.6 0.1 broadcast_in_dim.57
  169.7 0.0 copy-done.2
  169.7 0.7 select_reduce_fusion
  170.4 1.2 convolution_convert_fusion.2
  171.6 0.0 copy-done.1
  (10 shorter events, 0.2 us)
Async XLA Ops:
  7.2 2.3 %copy-start = (bf16[384,128]{1,0:T(8,128)(2,1)S(1)}, bf16[384,128]{1,0:T(8,128)(2,1)}, u32[]{:S(2)}) copy-start(bf16[384,128]{1,0:T(8,128)(2,1)} %param.7) | copy-start | bytes 294916
  7.2 44.2 %all-gather.5.cloned.1.call-start = ((), (), s32[]{:S(2)}) async-start(), calls=%async_computation.5 | async-start | bytes 2211840 | tf_op jit(solution)/shard_map/all_gather | solution.py:54
  24.5 56.4 %all-gather.3.cloned.1.call-start = ((), (), s32[]{:S(2)}) async-start(), calls=%async_computation.4 | async-start | bytes 2211840 | tf_op jit(solution)/shard_map/all_gather | solution.py:55
  51.4 9.4 %copy-start.3 = (bf16[3072,320]{0,1:T(8,128)(2,1)S(1)}, bf16[3072,320]{0,1:T(8,128)(2,1)}, u32[]{:S(2)}) copy-start(bf16[3072,320]{0,1:T(8,128)(2,1)} %all-gather.5.cloned.1.call-done) | copy-start | bytes 5898244
  154.1 17.5 %copy-start.1 = (bf16[384,128]{1,0:T(8,128)(2,1)S(1)}, bf16[384,128]{1,0:T(8,128)(2,1)}, u32[]{:S(2)}) copy-start(bf16[384,128]{1,0:T(8,128)(2,1)} %param.7) | copy-start | bytes 294916
  154.5 15.2 %copy-start.2 = (f32[128,2]{0,1:T(2,128)S(1)}, f32[128,2]{0,1:T(2,128)}, u32[]{:S(2)}) copy-start(f32[128,2]{0,1:T(2,128)} %param.10) | copy-start | bytes 3076
Sparse Core Ops, SparseCore 0:
  24.7 26.7 all-gather.4
  53.3 27.6 all-gather.2
where the time goes:
time: 179 us; the launch traced here: 178 us
  blocking collectives  73 us (41%)
  matrix products  57.8 us (32%)
  waiting for transfers between devices  26.3 us (15%)
  between operations  14.2 us (8%)
  other arithmetic  3.87 us (2%)
  local copies, waits for them, and re-layouts  3.26 us (2%)
    all_to_all x1, blocking collectives, body(): lax.all_to_all(jnp.concatenate([blocks, extra], axis=1), 'tensor', split_...  33 us
    all_gather x1, waiting for transfers between devices, body(): feature_piece = lax.all_gather(recv_in, 'tensor', axis=0, tiled=True)  14.9 us
    all_to_all x1, blocking collectives, body(): lax.all_to_all(send_in, 'expert', split_axis=1, concat_axis=1, tiled=True)  14.7 us
    all_to_all x1, blocking collectives, body(): lax.all_to_all(summed, 'expert', split_axis=1, concat_axis=1, tiled=True)  14.5 us
    dot_general x1, matrix products, body(): lax.dot_general(gate_rows, grad_gate, hidden_dims, preferred_element_type...  12.8 us
    dot_general x1, matrix products, body(): lax.dot_general(up_rows, grad_up, hidden_dims, preferred_element_type=jnp...  12.1 us
    dot_general x1, matrix products, body(): lax.dot_general(grad_piece, down_local, down_dims, preferred_element_type...  12 us
    all_gather x1, waiting for transfers between devices, body(): grad_piece = lax.all_gather(recv_grad, 'tensor', axis=0, tiled=True)  11.3 us
  transfers between devices with their start and end apart: 2, of which 2 were waited for; matrix products, arithmetic and copies ran while one was open for 11% of the time, Pallas kernels for 0%

commit v1 on v0

--- a/solution.py
+++ b/solution.py
@@ -4,6 +4,28 @@
 from jax.sharding import PartitionSpec as P
 
 EXTRA_ROWS = 16
+
+
+def turns_press(x_local):
+    y1 = lax.axis_size("expert")
+    piece_out = lax.axis_index("expert")
+    work_now, odd = (y1, piece_out)
+    far_arr = x_local.shape[1] // work_now
+    main = list(x_local.shape)
+    main[1] = far_arr
+    v_next = main[1]
+    main[1] = v_next * work_now
+    upper = jnp.zeros(main, x_local.dtype)
+    k0 = 0
+    while k0 < work_now:
+        current_block = lax.dynamic_slice_in_dim(x_local, (odd ^ k0) * far_arr, far_arr, axis=1)
+        if k0:
+            current_block = lax.ppermute(
+                current_block, "expert", [(j0, j0 ^ k0) for j0 in range(work_now)]
+            )
+        upper = lax.dynamic_update_slice_in_dim(upper, current_block, (odd ^ k0) * v_next, axis=1)
+        k0 += 1
+    return upper
 
 
 def slot_numbers(route_ids, expert_count, capacity):
@@ -49,7 +71,7 @@
     send_grad = jnp.dot(cotangent, placing, preferred_element_type=jnp.float32).astype(jnp.bfloat16)
     recv_in, recv_grad = (
         lax.all_to_all(send_in, "expert", split_axis=1, concat_axis=1, tiled=True),
-        lax.all_to_all(send_grad, "expert", split_axis=1, concat_axis=1, tiled=True),
+        turns_press(send_grad),
     )
     feature_piece = lax.all_gather(recv_in, "tensor", axis=0, tiled=True)
     grad_piece = lax.all_gather(recv_grad, "tensor", axis=0, tiled=True)

time: 179 us -> 179 us (level)
  blocking collectives: 73 us -> 62.2 us
  waiting for transfers between devices: 26.3 us -> 31.7 us
  starting transfers between devices: 0.08 us -> 4.53 us
    all_to_all x1 -> x0, blocking collectives: 10.7 us -> none  [body(): lax.all_to_all(send_grad, 'expert', split_axis=1, concat_axis=1, tiled=True)]
    ppermute x0 -> x3, starting transfers between devices: none -> 4.45 us  [turns_press(): lax.ppermute(current_block, 'expert', [(j0, j0 ^ k0) for j0 in range(work...]
    ppermute x0 -> x3, waiting for transfers between devices: none -> 3.55 us  [turns_press(): lax.ppermute(current_block, 'expert', [(j0, j0 ^ k0) for j0 in range(work...]
    all_gather x1, waiting for transfers between devices: 14.9 us -> 16.8 us  [body(): feature_piece = lax.all_gather(recv_in, 'tensor', axis=0, tiled=True)]
  transfers between devices with their start and end apart: 2 -> 5, of which waited for: 2 -> 4; matrix products, arithmetic and copies ran while one was open for 11% -> 11% of each run, Pallas kernels for 0% -> 0%
where the time goes in v1:
time: 179 us; the launch traced here: 178 us
  blocking collectives  62.2 us (35%)
  matrix products  57.8 us (32%)
  waiting for transfers between devices  31.7 us (18%)
  between operations  14.2 us (8%)
  starting transfers between devices  4.53 us (3%)
  local copies, waits for them, and re-layouts  4.08 us (2%)
  other arithmetic  3.87 us (2%)
    all_to_all x1, blocking collectives, body(): lax.all_to_all(jnp.concatenate([blocks, extra], axis=1), 'tensor', split_...  33 us
    all_gather x1, waiting for transfers between devices, body(): feature_piece = lax.all_gather(recv_in, 'tensor', axis=0, tiled=True)  16.8 us
    all_to_all x1, blocking collectives, body(): lax.all_to_all(send_in, 'expert', split_axis=1, concat_axis=1, tiled=True)  14.7 us
    all_to_all x1, blocking collectives, body(): lax.all_to_all(summed, 'expert', split_axis=1, concat_axis=1, tiled=True)  14.5 us
    dot_general x1, matrix products, body(): lax.dot_general(gate_rows, grad_gate, hidden_dims, preferred_element_type...  12.8 us
    dot_general x1, matrix products, body(): lax.dot_general(up_rows, grad_up, hidden_dims, preferred_element_type=jnp...  12.1 us
    dot_general x1, matrix products, body(): lax.dot_general(grad_piece, down_local, down_dims, preferred_element_type...  12 us
    all_gather x1, waiting for transfers between devices, body(): grad_piece = lax.all_gather(recv_grad, 'tensor', axis=0, tiled=True)  11.3 us
  transfers between devices with their start and end apart: 5, of which 4 were waited for; matrix products, arithmetic and copies ran while one was open for 11% of the time, Pallas kernels for 0%

profile of v1, /device:TPU:0, one launch (start us, length us, event | category | flops | bytes accessed | tf_op | source)
XLA Modules:
  0.0 178.5 jit_solution(17193575185479264435)
XLA Ops:
  7.2 0.0 copy-start
  7.2 0.0 all-gather.5.cloned.1.call-start
  7.2 0.7 convert_reduce_fusion.2
  7.9 0.1 fusion.23
  8.1 0.7 select_reduce_fusion.2
  8.8 0.7 convert_add_fusion
  9.5 0.0 copy-done
  9.5 0.2 convolution_convert_fusion
  9.8 14.7 %all_to_all.26 = bf16[384,4,80]{0,2,1:T(8,128)(2,1)} all-to-all(bf16[384,4,80]{0,2,1:T(8,128)(2,1)S(1)} %bitcast.52), channel_id=1, replica_groups=mesh['expert'=4,'tensor'=8] {'expert'}, dimensions={1} | all-to-all | bytes 491520 | tf_op jit(solution)/shard_map/all_to_all | solution.py:73
  24.5 0.0 all-gather.5.cloned.1.call-update
  24.5 0.0 all-gather.3.cloned.1.call-start
  24.6 1.1 convolution_convert_fusion.1
  25.8 0.3 collective-permute-start
  26.1 1.8 collective-permute-start.1
  27.9 2.4 %collective-permute-start.2 = (bf16[384,80]{0,1:T(8,128)(2,1)S(1)}, bf16[384,80]{0,1:T(8,128)(2,1)S(1)}, u32[]{:S(2)}, u32[]{:S(2)}) collective-permute-start(bf16[384,80]{0,1:T(8,128)(2,1)S(1)} %get-tuple-element.6), channel_id=1, source_target_pairs={{0,24},{8,16},{16,8},{24,0},{1,25},{9,17},{17,9},{25,1},{2,26},{10... | collective-permute-start | bytes 184328 | tf_op jit(solution)/shard_map/ppermute | solution.py:23
  30.3 0.0 collective-permute-done
  30.3 2.2 %collective-permute-done.1 = bf16[384,80]{0,1:T(8,128)(2,1)S(1)} collective-permute-done((bf16[384,80]{0,1:T(8,128)(2,1)S(1)}, bf16[384,80]{0,1:T(8,128)(2,1)S(1)}, u32[]{:S(2)}, u32[]{:S(2)}) %collective-permute-start.1) | collective-permute-done | bytes 61472 | tf_op jit(solution)/shard_map/ppermute | solution.py:23
  32.6 1.3 collective-permute-done.2
  33.9 0.0 copy-start.2
  33.9 0.7 copy-done.2
  34.6 0.0 all-gather.3.cloned.1.call-update
  34.6 16.8 %all-gather.5.cloned.1.call-done = bf16[3072,320]{0,1:T(8,128)(2,1)} async-done(((bf16[384,320]{0,1:T(8,128)(2,1)}), bf16[3072,320]{0,1:T(8,128)(2,1)}) %all-gather.5.cloned.1.call-update) | async-done | bytes 1966096 | tf_op jit(solution)/shard_map/all_gather | solution.py:76
  51.4 0.0 copy-start.4
  51.4 9.4 %fusion.2 = f32[320,2048]{1,0:T(8,128)S(1)} fusion(bf16[3072,320]{0,1:T(8,128)(2,1)} %all-gather.5.cloned.1.call-done, bf16[1,3072,2048]{2,1,0:T(8,128)(2,1)} %param.11), kind=kOutput, calls=%fused_computation.2 | convolution fusion | flops 4026531840 | bytes 17170432 | tf_op jit(solution)/shard_map/dot_general | solution.py:80
  60.8 0.0 copy-done.4
  60.8 8.8 %fusion.6 = f32[320,2048]{1,0:T(8,128)} fusion(bf16[3072,320]{0,1:T(8,128)(2,1)S(1)} %copy-done.4, bf16[1,3072,2048]{2,1,0:T(8,128)(2,1)} %param.12), kind=kOutput, calls=%fused_computation.6 | convolution fusion | flops 4026531840 | bytes 17170432 | tf_op jit(solution)/shard_map/dot_general | solution.py:83
  69.6 11.3 %all-gather.3.cloned.1.call-done = bf16[3072,320]{0,1:T(8,128)(2,1)} async-done(((bf16[384,320]{0,1:T(8,128)(2,1)}), bf16[3072,320]{0,1:T(8,128)(2,1)}) %all-gather.3.cloned.1.call-update) | async-done | bytes 1966096 | tf_op jit(solution)/shard_map/all_gather | solution.py:77
  80.9 12.0 %multiply_reduce_fusion = (f32[320]{0:T(512)S(1)}, f32[320,2048]{1,0:T(8,128)}) fusion(f32[320,2048]{1,0:T(8,128)} %fusion.6, f32[320,2048]{1,0:T(8,128)S(1)} %fusion.2, bf16[3072,320]{0,1:T(8,128)(2,1)} %all-gather.3.cloned.1.call-done, bf16[1,2048,3072]{2,1,0:T(8,128)(2,1)} %param.13), kind=kOutput, calls=%fused_computation.14 | convolution fusion | flops 4031119104 | bytes 22414592 | tf_op jit(solution)/shard_map/dot_general | solution.py:84
  93.0 12.8 %fusion = f32[320,3072]{1,0:T(8,128)} fusion(bf16[1,3072,2048]{2,1,0:T(8,128)(2,1)} %param.11, f32[320,2048]{1,0:T(8,128)S(1)} %fusion.2, f32[320,2048]{1,0:T(8,128)} %get-tuple-element.10, f32[320,2048]{1,0:T(8,128)} %fusion.6), kind=kOutput, calls=%fused_computation | convolution fusion | flops 4033085440 | bytes 24379392 | tf_op jit(solution)/shard_map/dot_general | solution.py:91
  105.8 12.1 %fusion.16 = bf16[3072,320]{0,1:T(8,128)(2,1)} fusion(f32[320,3072]{1,0:T(8,128)} %fusion, bf16[1,3072,2048]{2,1,0:T(8,128)(2,1)} %param.12, f32[320,2048]{1,0:T(8,128)} %get-tuple-element.10, f32[320,2048]{1,0:T(8,128)S(1)} %fusion.2), kind=kOutput, calls=%fused_computation.13 | convolution fusion | flops 4032430080 | bytes 23724032 | tf_op jit(solution)/shard_map/dot_general | solution.py:92
  117.9 2.9 %copy.40 = bf16[3072,320]{1,0:T(8,128)(2,1)S(1)} copy(bf16[3072,320]{0,1:T(8,128)(2,1)} %fusion.16) | data formatting | bytes 3932160 | tf_op jit(solution)/shard_map/reshape | solution.py:104
  120.9 0.3 pad_maximum_fusion
  121.1 33.0 %all_to_all.27 = bf16[8,400,320]{2,1,0:T(8,128)(2,1)S(1)} all-to-all(bf16[8,400,320]{2,1,0:T(8,128)(2,1)S(1)} %pad_maximum_fusion), channel_id=1, replica_groups=mesh['expert'=4,'tensor'=8] {'tensor'}, dimensions={0} | all-to-all | bytes 4096000 | tf_op jit(solution)/shard_map/all_to_all | solution.py:106
  154.1 0.0 copy-start.1
  154.1 0.4 convert_reduce_fusion
  154.5 0.0 copy-start.3
  154.7 0.2 copy.39
  154.8 14.5 %all_to_all.28 = bf16[400,4,80]{0,2,1:T(8,128)(2,1)S(1)} all-to-all(bf16[400,4,80]{0,2,1:T(8,128)(2,1)S(1)} %bitcast.49), channel_id=1, replica_groups=mesh['expert'=4,'tensor'=8] {'expert'}, dimensions={1} | all-to-all | bytes 512000 | tf_op jit(solution)/shard_map/all_to_all | solution.py:124
  169.3 0.1 convert_element_type.112
  169.4 0.2 fusion.22
  169.6 0.1 broadcast_in_dim.61
  169.7 0.0 copy-done.3
  169.7 0.7 select_reduce_fusion
  170.4 1.2 convolution_convert_fusion.2
  171.6 0.0 copy-done.1
  (16 shorter events, 0.3 us)
Async XLA Ops:
  7.2 2.3 %copy-start = (bf16[384,128]{1,0:T(8,128)(2,1)S(1)}, bf16[384,128]{1,0:T(8,128)(2,1)}, u32[]{:S(2)}) copy-start(bf16[384,128]{1,0:T(8,128)(2,1)} %param.7) | copy-start | bytes 294916
  7.2 44.2 %all-gather.5.cloned.1.call-start = ((), (), s32[]{:S(2)}) async-start(), calls=%async_computation.4 | async-start | bytes 2211840 | tf_op jit(solution)/shard_map/all_gather | solution.py:76
  24.5 56.4 %all-gather.3.cloned.1.call-start = ((), (), s32[]{:S(2)}) async-start(), calls=%async_computation.3 | async-start | bytes 2211840 | tf_op jit(solution)/shard_map/all_gather | solution.py:77
  25.8 4.5 %collective-permute-start = (bf16[384,80]{0,1:T(8,128)(2,1)S(1)}, bf16[384,80]{0,1:T(8,128)(2,1)S(1)}, u32[]{:S(2)}, u32[]{:S(2)}) collective-permute-start(bf16[384,80]{0,1:T(8,128)(2,1)S(1)} %get-tuple-element.8), channel_id=1, source_target_pairs={{0,8},{8,0},{16,24},{24,16},{1,9},{9,1},{17,25},{25,17},{2,10},{10... | collective-permute-start | bytes 184328 | tf_op jit(solution)/shard_map/ppermute | solution.py:23
  26.1 6.4 %collective-permute-start.1 = (bf16[384,80]{0,1:T(8,128)(2,1)S(1)}, bf16[384,80]{0,1:T(8,128)(2,1)S(1)}, u32[]{:S(2)}, u32[]{:S(2)}) collective-permute-start(bf16[384,80]{0,1:T(8,128)(2,1)S(1)} %get-tuple-element.7), channel_id=1, source_target_pairs={{0,16},{8,24},{16,0},{24,8},{1,17},{9,25},{17,1},{25,9},{2,18},{10... | collective-permute-start | bytes 184328 | tf_op jit(solution)/shard_map/ppermute | solution.py:23
  27.9 6.0 %collective-permute-start.2 = (bf16[384,80]{0,1:T(8,128)(2,1)S(1)}, bf16[384,80]{0,1:T(8,128)(2,1)S(1)}, u32[]{:S(2)}, u32[]{:S(2)}) collective-permute-start(bf16[384,80]{0,1:T(8,128)(2,1)S(1)} %get-tuple-element.6), channel_id=1, source_target_pairs={{0,24},{8,16},{16,8},{24,0},{1,25},{9,17},{17,9},{25,1},{2,26},{10... | collective-permute-start | bytes 184328 | tf_op jit(solution)/shard_map/ppermute | solution.py:23
  33.9 0.7 copy-start.2
  51.4 9.4 %copy-start.4 = (bf16[3072,320]{0,1:T(8,128)(2,1)S(1)}, bf16[3072,320]{0,1:T(8,128)(2,1)}, u32[]{:S(2)}) copy-start(bf16[3072,320]{0,1:T(8,128)(2,1)} %all-gather.5.cloned.1.call-done) | copy-start | bytes 5898244
  154.1 17.5 %copy-start.1 = (bf16[384,128]{1,0:T(8,128)(2,1)S(1)}, bf16[384,128]{1,0:T(8,128)(2,1)}, u32[]{:S(2)}) copy-start(bf16[384,128]{1,0:T(8,128)(2,1)} %param.7) | copy-start | bytes 294916
  154.5 15.2 %copy-start.3 = (f32[128,2]{0,1:T(2,128)S(1)}, f32[128,2]{0,1:T(2,128)}, u32[]{:S(2)}) copy-start(f32[128,2]{0,1:T(2,128)} %param.10) | copy-start | bytes 3076
Sparse Core Ops, SparseCore 0:
  24.7 26.7 all-gather.4
  53.3 27.6 all-gather.2
